TPU v7x, 256 devices: a whole 4x4x8 slice. The times are simulated.
256 devices in a mesh: ctx: 32 (over z, y_hi, core), tp: 8 (over y_lo, x).
Axes of the slice: x: 4, y: 4 (y_hi: 2, y_lo: 2; y = y_hi * 2 + y_lo), z: 8, core: 2. Of those that a mesh axis runs over, the one named last changes fastest.
Arguments:
- queries: bfloat16 [16384, 8192], P('ctx', 'tp'), may hold values from -132 to 132
- keys: bfloat16 [16384, 1024], P('ctx', 'tp'), may hold values from -6 to 6
- values: bfloat16 [16384, 1024], P('ctx', 'tp'), may hold values from -6 to 6
- prefix_spans: int32 [32], P('ctx'), may hold values from 1 to 7, as said below
Outputs:
- attended: bfloat16 [16384, 8192], P('ctx', 'tp')
Inputs may be any that keep to these rules, and one draw needn't show every extreme that they name: `prefix_spans`: 7 is reached by some block in every draw.
All inputs are finite; a program needn't handle non-finite values.
Results may differ from a plain program's by a relative error of at most 0.003.
Values may be sent and summed in bfloat16 or wider, within the bound.
A program may use at most 128 MiB of HBM per device.

v0:
```python
import math

import jax
import jax.numpy as jnp
from jax import lax
from jax.sharding import PartitionSpec as P

QUERY_HEAD_COUNT = 64
KEY_VALUE_HEADS = 8
HEAD_SIZE = 128
PREFIX_BLOCK_MAX = 7


def passed_along(shard, axis, by):
    length = lax.axis_size(axis)
    pairs = [(i, i + by) for i in range(length) if 0 <= i + by < length]
    return lax.ppermute(shard, axis, pairs)


def block_update(running_state, scores, piece_values):
    running_max, total, acc = running_state
    new_max = jnp.maximum(running_max, jnp.max(scores, axis=-1))
    correct = jnp.exp(running_max - new_max)
    probs = jnp.exp(scores - new_max[..., None])
    total = total * correct + jnp.sum(probs, axis=-1)
    weights = probs.astype(jnp.bfloat16)
    acc = acc * correct[..., None] + jnp.einsum(
        "rhgt,thd->rhgd", weights, piece_values, preferred_element_type=jnp.float32
    )
    return (new_max, total, acc)


def on_device(queries, keys, values, prefix_spans):
    rows = queries.shape[0]
    kv_local = keys.shape[1] // HEAD_SIZE
    query_group = QUERY_HEAD_COUNT // KEY_VALUE_HEADS
    scale = 1.0 / math.sqrt(HEAD_SIZE)
    own = jnp.stack([keys, values])
    pieces = []
    carried = own
    for step in range(PREFIX_BLOCK_MAX):
        carried = passed_along(carried, "ctx", 1)
        pieces.append(carried)
    query_head_rows = queries.reshape(rows, kv_local, query_group, HEAD_SIZE)
    position = lax.axis_index("ctx")
    limit = prefix_spans[0]
    row_ids = lax.broadcasted_iota(jnp.int32, (rows, 1, 1, rows), 0)
    col_ids = lax.broadcasted_iota(jnp.int32, (rows, 1, 1, rows), 3)
    running_state = (
        jnp.full((rows, kv_local, query_group), -jnp.inf, jnp.float32),
        jnp.zeros((rows, kv_local, query_group), jnp.float32),
        jnp.zeros((rows, kv_local, query_group, HEAD_SIZE), jnp.float32),
    )
    for step in range(PREFIX_BLOCK_MAX + 1):
        piece = own if step == 0 else pieces[step - 1]
        piece_keys = piece[0].reshape(rows, kv_local, HEAD_SIZE)
        piece_values = piece[1].reshape(rows, kv_local, HEAD_SIZE)
        scores = (
            jnp.einsum(
                "rhgd,thd->rhgt", query_head_rows, piece_keys, preferred_element_type=jnp.float32
            )
            * scale
        )
        if step == 0:
            admitted = row_ids >= col_ids
        else:
            admitted = jnp.logical_and(step <= limit, position - step >= 0)
        scores = jnp.where(admitted, scores, -jnp.inf)
        running_state = block_update(running_state, scores, piece_values)
    output = running_state[2] / running_state[1][..., None]
    return output.reshape(rows, kv_local * query_group * HEAD_SIZE).astype(jnp.bfloat16)


def solution(mesh):
    placed = (P("ctx", "tp"), P("ctx", "tp"), P("ctx", "tp"), P("ctx"))
    return jax.shard_map(
        on_device, mesh=mesh, in_specs=placed, out_specs=P("ctx", "tp"), check_vma=False
    )
```

profile of v0, /device:TPU:142, one launch (start us, length us, event | category | flops | bytes accessed | tf_op | source)
XLA Modules:
  0.0 139.5 jit_solution(14795854347166191239)
XLA Ops:
  1.1 1.9 %collective-permute-start = (bf16[2,512,128]{2,1,0:T(8,128)(2,1)S(1)}, bf16[2,512,128]{2,1,0:T(8,128)(2,1)S(1)}, u32[]{:S(2)}, u32[]{:S(2)}) collective-permute-start(bf16[2,512,128]{2,1,0:T(8,128)(2,1)S(1)} %pad_maximum_fusion), channel_id=1, source_target_pairs={{0,8},{8,16},{16,24},{24,32},{32,40},{40,48},{48,56},{56,64},{64,7... | collective-permute-start | bytes 786440 | tf_op jit(solution)/shard_map/ppermute | solution.py:17
  3.1 2.4 %fusion.23 = (f32[512,8]{0,1:T(8,128)S(1)}, f32[512,512,8]{1,0,2:T(8,128)S(1)}) fusion(pred[512,512]{0,1:T(8,128)(4,1)S(1)} %iota_compare_fusion, bf16[512,128]{1,0:T(8,128)(2,1)} %param.5, bf16[512,1024]{1,0:T(8,128)(2,1)S(1)} %copy-done), kind=kOutput, calls=%fused_computation.46 | convolution fusion | flops 543158272 | bytes 9846784 | tf_op jit(solution)/shard_map/rhgd,thd->rhgt/dot_general | solution.py:59
  5.5 3.2 %copy-done.2 = f32[512,512,8]{1,0,2:T(8,128)} copy-done((f32[512,512,8]{1,0,2:T(8,128)}, f32[512,512,8]{1,0,2:T(8,128)S(1)}, u32[]{:S(2)}) %copy-start.2) | copy-done | bytes 8388632
  8.7 3.4 %fusion.32 = f32[512,8,128]{0,2,1:T(8,128)} fusion(f32[512,512,8]{1,0,2:T(8,128)S(1)} %get-tuple-element.34, f32[512,8]{0,1:T(8,128)S(1)} %get-tuple-element.33, pred[512,512]{0,1:T(8,128)(4,1)S(1)} %iota_compare_fusion, bf16[512,128]{1,0:T(8,128)(2,1)S(1)} %copy-done.16), kind=kOutput, calls=%fused_computation.55 | convolution fusion | flops 545259520 | bytes 10895360 | tf_op jit(solution)/shard_map/rhgt,thd->rhgd/dot_general | solution.py:27
  12.8 4.3 %collective-permute-start.1 = (bf16[2,512,128]{2,1,0:T(8,128)(2,1)S(1)}, bf16[2,512,128]{2,1,0:T(8,128)(2,1)S(1)}, u32[]{:S(2)}, u32[]{:S(2)}) collective-permute-start(bf16[2,512,128]{2,1,0:T(8,128)(2,1)S(1)} %collective-permute-done), channel_id=1, source_target_pairs={{0,8},{8,16},{16,24},{24,32},{32,40},{40,48},{48,56},{56,64},{64,7... | collective-permute-start | bytes 786440 | tf_op jit(solution)/shard_map/ppermute | solution.py:17
  18.4 5.7 %collective-permute-done.1 = bf16[2,512,128]{2,1,0:T(8,128)(2,1)S(1)} collective-permute-done((bf16[2,512,128]{2,1,0:T(8,128)(2,1)S(1)}, bf16[2,512,128]{2,1,0:T(8,128)(2,1)S(1)}, u32[]{:S(2)}, u32[]{:S(2)}) %collective-permute-start.1) | collective-permute-done | bytes 262176 | tf_op jit(solution)/shard_map/ppermute | solution.py:17
  24.1 1.9 %collective-permute-start.2 = (bf16[2,512,128]{2,1,0:T(8,128)(2,1)S(1)}, bf16[2,512,128]{2,1,0:T(8,128)(2,1)S(1)}, u32[]{:S(2)}, u32[]{:S(2)}) collective-permute-start(bf16[2,512,128]{2,1,0:T(8,128)(2,1)S(1)} %collective-permute-done.1), channel_id=1, source_target_pairs={{0,8},{8,16},{16,24},{24,32},{32,40},{40,48},{48,56},{56,64},{64,7... | collective-permute-start | bytes 786440 | tf_op jit(solution)/shard_map/ppermute | solution.py:17
  27.3 8.1 %collective-permute-done.2 = bf16[2,512,128]{2,1,0:T(8,128)(2,1)S(1)} collective-permute-done((bf16[2,512,128]{2,1,0:T(8,128)(2,1)S(1)}, bf16[2,512,128]{2,1,0:T(8,128)(2,1)S(1)}, u32[]{:S(2)}, u32[]{:S(2)}) %collective-permute-start.2) | collective-permute-done | bytes 262176 | tf_op jit(solution)/shard_map/ppermute | solution.py:17
  35.4 1.9 %collective-permute-start.3 = (bf16[2,512,128]{2,1,0:T(8,128)(2,1)S(1)}, bf16[2,512,128]{2,1,0:T(8,128)(2,1)S(1)}, u32[]{:S(2)}, u32[]{:S(2)}) collective-permute-start(bf16[2,512,128]{2,1,0:T(8,128)(2,1)S(1)} %collective-permute-done.2), channel_id=1, source_target_pairs={{0,8},{8,16},{16,24},{24,32},{32,40},{40,48},{48,56},{56,64},{64,7... | collective-permute-start | bytes 786440 | tf_op jit(solution)/shard_map/ppermute | solution.py:17
  38.7 8.1 %collective-permute-done.3 = bf16[2,512,128]{2,1,0:T(8,128)(2,1)S(1)} collective-permute-done((bf16[2,512,128]{2,1,0:T(8,128)(2,1)S(1)}, bf16[2,512,128]{2,1,0:T(8,128)(2,1)S(1)}, u32[]{:S(2)}, u32[]{:S(2)}) %collective-permute-start.3) | collective-permute-done | bytes 262176 | tf_op jit(solution)/shard_map/ppermute | solution.py:17
  46.7 1.9 %collective-permute-start.4 = (bf16[2,512,128]{2,1,0:T(8,128)(2,1)S(1)}, bf16[2,512,128]{2,1,0:T(8,128)(2,1)S(1)}, u32[]{:S(2)}, u32[]{:S(2)}) collective-permute-start(bf16[2,512,128]{2,1,0:T(8,128)(2,1)S(1)} %collective-permute-done.3), channel_id=1, source_target_pairs={{0,8},{8,16},{16,24},{24,32},{32,40},{40,48},{48,56},{56,64},{64,7... | collective-permute-start | bytes 786440 | tf_op jit(solution)/shard_map/ppermute | solution.py:17
  48.7 4.5 %bitcast_reduce_fusion.3 = (f32[512,8]{0,1:T(8,128)S(1)}, f32[512,512,8]{1,0,2:T(8,128)}) fusion(pred[]{:T(512)S(6)} %and.25, bf16[2,512,128]{2,1,0:T(8,128)(2,1)S(1)} %collective-permute-done.3, bf16[512,1024]{1,0:T(8,128)(2,1)S(1)} %copy-done), kind=kOutput, calls=%fused_computation.11 | convolution fusion | flops 543158272 | bytes 9584641 | tf_op jit(solution)/shard_map/rhgd,thd->rhgt/dot_general | solution.py:59
  53.1 4.9 %collective-permute-done.4 = bf16[2,512,128]{2,1,0:T(8,128)(2,1)S(1)} collective-permute-done((bf16[2,512,128]{2,1,0:T(8,128)(2,1)S(1)}, bf16[2,512,128]{2,1,0:T(8,128)(2,1)S(1)}, u32[]{:S(2)}, u32[]{:S(2)}) %collective-permute-start.4) | collective-permute-done | bytes 262176 | tf_op jit(solution)/shard_map/ppermute | solution.py:17
  58.0 1.9 %collective-permute-start.5 = (bf16[2,512,128]{2,1,0:T(8,128)(2,1)S(1)}, bf16[2,512,128]{2,1,0:T(8,128)(2,1)S(1)}, u32[]{:S(2)}, u32[]{:S(2)}) collective-permute-start(bf16[2,512,128]{2,1,0:T(8,128)(2,1)S(1)} %collective-permute-done.4), channel_id=1, source_target_pairs={{0,8},{8,16},{16,24},{24,32},{32,40},{40,48},{48,56},{56,64},{64,7... | collective-permute-start | bytes 786440 | tf_op jit(solution)/shard_map/ppermute | solution.py:17
  60.0 4.5 %bitcast_reduce_fusion.2 = (f32[512,8]{0,1:T(8,128)S(1)}, f32[512,512,8]{1,0,2:T(8,128)}) fusion(pred[]{:T(512)S(6)} %and.26, bf16[2,512,128]{2,1,0:T(8,128)(2,1)S(1)} %collective-permute-done.4, bf16[512,1024]{1,0:T(8,128)(2,1)S(1)} %copy-done), kind=kOutput, calls=%fused_computation.8 | convolution fusion | flops 543158272 | bytes 9584641 | tf_op jit(solution)/shard_map/rhgd,thd->rhgt/dot_general | solution.py:59
  64.4 4.9 %collective-permute-done.5 = bf16[2,512,128]{2,1,0:T(8,128)(2,1)S(1)} collective-permute-done((bf16[2,512,128]{2,1,0:T(8,128)(2,1)S(1)}, bf16[2,512,128]{2,1,0:T(8,128)(2,1)S(1)}, u32[]{:S(2)}, u32[]{:S(2)}) %collective-permute-start.5) | collective-permute-done | bytes 262176 | tf_op jit(solution)/shard_map/ppermute | solution.py:17
  69.3 2.1 %collective-permute-start.6 = (bf16[2,512,128]{2,1,0:T(8,128)(2,1)S(1)}, bf16[2,512,128]{2,1,0:T(8,128)(2,1)S(1)}, u32[]{:S(2)}, u32[]{:S(2)}) collective-permute-start(bf16[2,512,128]{2,1,0:T(8,128)(2,1)S(1)} %collective-permute-done.5), channel_id=1, source_target_pairs={{0,8},{8,16},{16,24},{24,32},{32,40},{40,48},{48,56},{56,64},{64,7... | collective-permute-start | bytes 786440 | tf_op jit(solution)/shard_map/ppermute | solution.py:17
  71.4 4.5 %bitcast_reduce_fusion.1 = (f32[512,8]{0,1:T(8,128)S(1)}, f32[512,512,8]{1,0,2:T(8,128)}) fusion(pred[]{:T(512)S(6)} %and.27, bf16[2,512,128]{2,1,0:T(8,128)(2,1)S(1)} %collective-permute-done.5, bf16[512,1024]{1,0:T(8,128)(2,1)S(1)} %copy-done), kind=kOutput, calls=%fused_computation.5 | convolution fusion | flops 543158272 | bytes 9584641 | tf_op jit(solution)/shard_map/rhgd,thd->rhgt/dot_general | solution.py:59
  75.9 4.7 %collective-permute-done.6 = bf16[2,512,128]{2,1,0:T(8,128)(2,1)S(1)} collective-permute-done((bf16[2,512,128]{2,1,0:T(8,128)(2,1)S(1)}, bf16[2,512,128]{2,1,0:T(8,128)(2,1)S(1)}, u32[]{:S(2)}, u32[]{:S(2)}) %collective-permute-start.6) | collective-permute-done | bytes 262176 | tf_op jit(solution)/shard_map/ppermute | solution.py:17
  80.6 4.5 %bitcast_reduce_fusion = (f32[512,8]{0,1:T(8,128)S(1)}, f32[512,512,8]{1,0,2:T(8,128)}) fusion(pred[]{:T(512)S(6)} %and.28, bf16[2,512,128]{2,1,0:T(8,128)(2,1)S(1)} %collective-permute-done.6, bf16[512,1024]{1,0:T(8,128)(2,1)S(1)} %copy-done), kind=kOutput, calls=%fused_computation.2 | convolution fusion | flops 543158272 | bytes 9584641 | tf_op jit(solution)/shard_map/rhgd,thd->rhgt/dot_general | solution.py:59
  85.1 7.7 %fusion.7 = (f32[512,8]{0,1:T(8,128)S(1)}, f32[512,8]{0,1:T(8,128)S(1)}) fusion(f32[512,512,8]{1,0,2:T(8,128)} %copy-done.2, f32[512,8]{0,1:T(8,128)S(1)} %get-tuple-element.33, pred[512,512]{0,1:T(8,128)(4,1)S(1)} %iota_compare_fusion, f32[512,8]{0,1:T(8,128)S(1)} %get-tuple-element.13, f32[512,512,8]{1,0,2:T(8,128)} %get-tuple-element.22, pred[]{:T(512)S(6)} %and.28), kind=kLoop, calls=%fused_computation.30 | loop fusion | flops 16769024 | bytes 17104896 | tf_op jit(solution)/shard_map/reduce_sum | solution.py:25
  92.8 7.6 %fusion.17 = (f32[512,8]{0,1:T(8,128)S(1)}, f32[512,8]{0,1:T(8,128)S(1)}) fusion(f32[512,512,8]{1,0,2:T(8,128)} %get-tuple-element.26, f32[512,8]{0,1:T(8,128)S(1)} %get-tuple-element.15, pred[]{:T(512)S(6)} %and.26, f32[512,8]{0,1:T(8,128)S(1)} %get-tuple-element.14, f32[512,512,8]{1,0,2:T(8,128)} %get-tuple-element.24, pred[]{:T(512)S(6)} %and.27), kind=kLoop, calls=%fused_computation.40 | loop fusion | flops 16769024 | bytes 16842754 | tf_op jit(solution)/shard_map/reduce_sum | solution.py:25
  100.5 3.3 %fusion.13 = (f32[512,8]{0,1:T(8,128)S(1)}, f32[512,8]{0,1:T(8,128)S(1)}) fusion(f32[512,512,8]{1,0,2:T(8,128)S(1)} %get-tuple-element.30, f32[512,8]{0,1:T(8,128)S(1)} %get-tuple-element.17, pred[]{:T(512)S(6)} %and.24, f32[512,8]{0,1:T(8,128)S(1)} %get-tuple-element.16, f32[512,512,8]{1,0,2:T(8,128)S(1)} %bitcast.359, pred[]{:T(512)S(6)} %and.25), kind=kLoop, calls=%fused_computation.36 | loop fusion | flops 16769024 | bytes 16842754 | tf_op jit(solution)/shard_map/reduce_sum | solution.py:25
  103.8 3.6 %fusion.9 = (f32[512,8]{0,1:T(8,128)S(1)}, f32[512,8]{0,1:T(8,128)S(1)}) fusion(f32[512,512,8]{1,0,2:T(8,128)S(1)} %get-tuple-element.36, f32[512,8]{0,1:T(8,128)S(1)} %get-tuple-element.19, pred[]{:T(512)S(6)} %and.22, f32[512,8]{0,1:T(8,128)S(1)} %get-tuple-element.18, f32[512,512,8]{1,0,2:T(8,128)S(1)} %get-tuple-element.32, pred[]{:T(512)S(6)} %and.23), kind=kLoop, calls=%fused_computation.32 | loop fusion | flops 16769024 | bytes 16842754 | tf_op jit(solution)/shard_map/reduce_sum | solution.py:25
  108.0 6.7 %fusion.44 = f32[128,512,8]{1,0,2:T(8,128)} fusion(f32[512,512,8]{1,0,2:T(8,128)} %get-tuple-element.24, f32[512,8]{0,1:T(8,128)S(1)} %get-tuple-element.14, pred[]{:T(512)S(6)} %and.27, bf16[2,512,128]{2,1,0:T(8,128)(2,1)S(1)} %copy-done.15), kind=kOutput, calls=%fused_computation.61 | convolution fusion | flops 545259520 | bytes 10633217 | tf_op jit(solution)/shard_map/rhgt,thd->rhgd/dot_general | solution.py:27
  114.7 6.7 %fusion.42 = f32[128,512,8]{1,0,2:T(8,128)} fusion(f32[512,512,8]{1,0,2:T(8,128)} %get-tuple-element.26, f32[512,8]{0,1:T(8,128)S(1)} %get-tuple-element.15, pred[]{:T(512)S(6)} %and.26, bf16[2,512,128]{2,1,0:T(8,128)(2,1)S(1)} %copy-done.13), kind=kOutput, calls=%fused_computation.60 | convolution fusion | flops 545259520 | bytes 10633217 | tf_op jit(solution)/shard_map/rhgt,thd->rhgd/dot_general | solution.py:27
  121.4 3.3 %fusion.40 = f32[128,512,8]{1,0,2:T(8,128)} fusion(f32[512,512,8]{1,0,2:T(8,128)S(1)} %bitcast.359, f32[512,8]{0,1:T(8,128)S(1)} %get-tuple-element.16, pred[]{:T(512)S(6)} %and.25, bf16[2,512,128]{2,1,0:T(8,128)(2,1)S(1)} %copy-done.11), kind=kOutput, calls=%fused_computation.59 | convolution fusion | flops 545259520 | bytes 10633217 | tf_op jit(solution)/shard_map/rhgt,thd->rhgd/dot_general | solution.py:27
  124.7 1.9 %fusion.38 = f32[128,512,8]{1,0,2:T(8,128)S(1)} fusion(f32[512,512,8]{1,0,2:T(8,128)S(1)} %get-tuple-element.30, f32[512,8]{0,1:T(8,128)S(1)} %get-tuple-element.17, pred[]{:T(512)S(6)} %and.24, bf16[2,512,128]{2,1,0:T(8,128)(2,1)S(1)} %copy-done.9), kind=kOutput, calls=%fused_computation.58 | convolution fusion | flops 545259520 | bytes 10633217 | tf_op jit(solution)/shard_map/rhgt,thd->rhgd/dot_general | solution.py:27
  126.7 1.9 %fusion.36 = f32[128,512,8]{1,0,2:T(8,128)S(1)} fusion(f32[512,512,8]{1,0,2:T(8,128)S(1)} %get-tuple-element.32, f32[512,8]{0,1:T(8,128)S(1)} %get-tuple-element.18, pred[]{:T(512)S(6)} %and.23, bf16[2,512,128]{2,1,0:T(8,128)(2,1)S(1)} %copy-done.7), kind=kOutput, calls=%fused_computation.57 | convolution fusion | flops 545259520 | bytes 10633217 | tf_op jit(solution)/shard_map/rhgt,thd->rhgd/dot_general | solution.py:27
  128.6 1.9 %fusion.34 = f32[128,512,8]{1,0,2:T(8,128)S(1)} fusion(f32[512,512,8]{1,0,2:T(8,128)S(1)} %get-tuple-element.36, f32[512,8]{0,1:T(8,128)S(1)} %get-tuple-element.19, pred[]{:T(512)S(6)} %and.22, bf16[2,512,128]{2,1,0:T(8,128)(2,1)S(1)} %collective-permute-done), kind=kOutput, calls=%fused_computation.56 | convolution fusion | flops 545259520 | bytes 10633217 | tf_op jit(solution)/shard_map/rhgt,thd->rhgd/dot_general | solution.py:27
  132.1 5.2 %bitcast_convert_fusion = bf16[512,1,8,128]{0,3,2,1:T(8,128)(2,1)} fusion(f32[128,512,8]{1,0,2:T(8,128)S(1)} %copy-done.3, f32[128,512,8]{1,0,2:T(8,128)S(1)} %copy-done.4, f32[128,512,8]{1,0,2:T(8,128)S(1)} %copy-done.5, f32[128,512,8]{1,0,2:T(8,128)S(1)} %fusion.38, f32[128,512,8]{1,0,2:T(8,128)S(1)} %fusion.36, f32[128,512,8]{1,0,2:T(8,128)S(1)} %fusion.34, ...), kind=kOutput, calls=%fused_computation.87 | convolution fusion | flops 554172416 | bytes 24412160 | tf_op jit(solution)/shard_map/rhgt,thd->rhgd/dot_general | solution.py:27
  137.3 2.3 %copy.29 = bf16[512,1024]{1,0:T(8,128)(2,1)} copy(bf16[512,1024]{0,1:T(8,128)(2,1)} %bitcast.362) | data formatting | bytes 2097152 | tf_op jit(solution)/shard_map/convert_element_type | solution.py:71
  (57 shorter events, 7.2 us)
Async XLA Ops:
  0.0 3.1 %copy-start = (bf16[512,1024]{1,0:T(8,128)(2,1)S(1)}, bf16[512,1024]{1,0:T(8,128)(2,1)}, u32[]{:S(2)}) copy-start(bf16[512,1024]{1,0:T(8,128)(2,1)} %param.4) | copy-start | bytes 3145732
  0.0 8.7 %copy-start.16 = (bf16[512,128]{1,0:T(8,128)(2,1)S(1)}, bf16[512,128]{1,0:T(8,128)(2,1)}, u32[]{:S(2)}) copy-start(bf16[512,128]{1,0:T(8,128)(2,1)} %param.6) | copy-start | bytes 393220
  1.1 11.7 %collective-permute-start = (bf16[2,512,128]{2,1,0:T(8,128)(2,1)S(1)}, bf16[2,512,128]{2,1,0:T(8,128)(2,1)S(1)}, u32[]{:S(2)}, u32[]{:S(2)}) collective-permute-start(bf16[2,512,128]{2,1,0:T(8,128)(2,1)S(1)} %pad_maximum_fusion), channel_id=1, source_target_pairs={{0,8},{8,16},{16,24},{24,32},{32,40},{40,48},{48,56},{56,64},{64,7... | collective-permute-start | bytes 786440 | tf_op jit(solution)/shard_map/ppermute | solution.py:17
  5.5 3.2 %copy-start.2 = (f32[512,512,8]{1,0,2:T(8,128)}, f32[512,512,8]{1,0,2:T(8,128)S(1)}, u32[]{:S(2)}) copy-start(f32[512,512,8]{1,0,2:T(8,128)S(1)} %get-tuple-element.34) | copy-start | bytes 25165828
  12.8 11.3 %collective-permute-start.1 = (bf16[2,512,128]{2,1,0:T(8,128)(2,1)S(1)}, bf16[2,512,128]{2,1,0:T(8,128)(2,1)S(1)}, u32[]{:S(2)}, u32[]{:S(2)}) collective-permute-start(bf16[2,512,128]{2,1,0:T(8,128)(2,1)S(1)} %collective-permute-done), channel_id=1, source_target_pairs={{0,8},{8,16},{16,24},{24,32},{32,40},{40,48},{48,56},{56,64},{64,7... | collective-permute-start | bytes 786440 | tf_op jit(solution)/shard_map/ppermute | solution.py:17
  24.1 14.5 %copy-start.6 = (bf16[2,512,128]{2,1,0:T(8,128)(2,1)}, bf16[2,512,128]{2,1,0:T(8,128)(2,1)S(1)}, u32[]{:S(2)}) copy-start(bf16[2,512,128]{2,1,0:T(8,128)(2,1)S(1)} %collective-permute-done.1) | copy-start | bytes 786436
  24.1 11.3 %collective-permute-start.2 = (bf16[2,512,128]{2,1,0:T(8,128)(2,1)S(1)}, bf16[2,512,128]{2,1,0:T(8,128)(2,1)S(1)}, u32[]{:S(2)}, u32[]{:S(2)}) collective-permute-start(bf16[2,512,128]{2,1,0:T(8,128)(2,1)S(1)} %collective-permute-done.1), channel_id=1, source_target_pairs={{0,8},{8,16},{16,24},{24,32},{32,40},{40,48},{48,56},{56,64},{64,7... | collective-permute-start | bytes 786440 | tf_op jit(solution)/shard_map/ppermute | solution.py:17
  35.4 17.7 %copy-start.8 = (bf16[2,512,128]{2,1,0:T(8,128)(2,1)}, bf16[2,512,128]{2,1,0:T(8,128)(2,1)S(1)}, u32[]{:S(2)}) copy-start(bf16[2,512,128]{2,1,0:T(8,128)(2,1)S(1)} %collective-permute-done.2) | copy-start | bytes 786436
  35.4 11.3 %collective-permute-start.3 = (bf16[2,512,128]{2,1,0:T(8,128)(2,1)S(1)}, bf16[2,512,128]{2,1,0:T(8,128)(2,1)S(1)}, u32[]{:S(2)}, u32[]{:S(2)}) collective-permute-start(bf16[2,512,128]{2,1,0:T(8,128)(2,1)S(1)} %collective-permute-done.2), channel_id=1, source_target_pairs={{0,8},{8,16},{16,24},{24,32},{32,40},{40,48},{48,56},{56,64},{64,7... | collective-permute-start | bytes 786440 | tf_op jit(solution)/shard_map/ppermute | solution.py:17
  46.7 17.7 %copy-start.10 = (bf16[2,512,128]{2,1,0:T(8,128)(2,1)}, bf16[2,512,128]{2,1,0:T(8,128)(2,1)S(1)}, u32[]{:S(2)}) copy-start(bf16[2,512,128]{2,1,0:T(8,128)(2,1)S(1)} %collective-permute-done.3) | copy-start | bytes 786436
  46.7 11.3 %collective-permute-start.4 = (bf16[2,512,128]{2,1,0:T(8,128)(2,1)S(1)}, bf16[2,512,128]{2,1,0:T(8,128)(2,1)S(1)}, u32[]{:S(2)}, u32[]{:S(2)}) collective-permute-start(bf16[2,512,128]{2,1,0:T(8,128)(2,1)S(1)} %collective-permute-done.3), channel_id=1, source_target_pairs={{0,8},{8,16},{16,24},{24,32},{32,40},{40,48},{48,56},{56,64},{64,7... | collective-permute-start | bytes 786440 | tf_op jit(solution)/shard_map/ppermute | solution.py:17
  58.0 17.9 %copy-start.12 = (bf16[2,512,128]{2,1,0:T(8,128)(2,1)}, bf16[2,512,128]{2,1,0:T(8,128)(2,1)S(1)}, u32[]{:S(2)}) copy-start(bf16[2,512,128]{2,1,0:T(8,128)(2,1)S(1)} %collective-permute-done.4) | copy-start | bytes 786436
  58.0 11.3 %collective-permute-start.5 = (bf16[2,512,128]{2,1,0:T(8,128)(2,1)S(1)}, bf16[2,512,128]{2,1,0:T(8,128)(2,1)S(1)}, u32[]{:S(2)}, u32[]{:S(2)}) collective-permute-start(bf16[2,512,128]{2,1,0:T(8,128)(2,1)S(1)} %collective-permute-done.4), channel_id=1, source_target_pairs={{0,8},{8,16},{16,24},{24,32},{32,40},{40,48},{48,56},{56,64},{64,7... | collective-permute-start | bytes 786440 | tf_op jit(solution)/shard_map/ppermute | solution.py:17
  69.3 6.6 %copy-start.14 = (bf16[2,512,128]{2,1,0:T(8,128)(2,1)}, bf16[2,512,128]{2,1,0:T(8,128)(2,1)S(1)}, u32[]{:S(2)}) copy-start(bf16[2,512,128]{2,1,0:T(8,128)(2,1)S(1)} %collective-permute-done.5) | copy-start | bytes 786436
  69.3 11.3 %collective-permute-start.6 = (bf16[2,512,128]{2,1,0:T(8,128)(2,1)S(1)}, bf16[2,512,128]{2,1,0:T(8,128)(2,1)S(1)}, u32[]{:S(2)}, u32[]{:S(2)}) collective-permute-start(bf16[2,512,128]{2,1,0:T(8,128)(2,1)S(1)} %collective-permute-done.5), channel_id=1, source_target_pairs={{0,8},{8,16},{16,24},{24,32},{32,40},{40,48},{48,56},{56,64},{64,7... | collective-permute-start | bytes 786440 | tf_op jit(solution)/shard_map/ppermute | solution.py:17
  80.6 4.5 %copy-start.17 = (bf16[2,512,128]{2,1,0:T(8,128)(2,1)}, bf16[2,512,128]{2,1,0:T(8,128)(2,1)S(1)}, u32[]{:S(2)}) copy-start(bf16[2,512,128]{2,1,0:T(8,128)(2,1)S(1)} %collective-permute-done.6) | copy-start | bytes 786436
  80.6 19.8 %slice-start = ((s8[8388608]{0:T(1024)(128)(4,1)}), s8[4194304]{0:T(1024)(128)(4,1)S(1)}, s32[]{:S(2)}) async-start(s8[8388608]{0:T(1024)(128)(4,1)} %bitcast.358), calls=%async_computation | async-start | bytes 8388608
  85.1 15.3 %slice-start.1 = ((s8[8388608]{0:T(1024)(128)(4,1)}), s8[4194304]{0:T(1024)(128)(4,1)S(1)}, s32[]{:S(2)}) async-start(s8[8388608]{0:T(1024)(128)(4,1)} %bitcast.358), calls=%async_computation.1 | async-start | bytes 8388608
  103.8 4.2 %copy-start.15 = (bf16[2,512,128]{2,1,0:T(8,128)(2,1)S(1)}, bf16[2,512,128]{2,1,0:T(8,128)(2,1)}, u32[]{:S(2)}) copy-start(bf16[2,512,128]{2,1,0:T(8,128)(2,1)} %copy-done.14) | copy-start | bytes 786436
  107.4 7.3 %copy-start.13 = (bf16[2,512,128]{2,1,0:T(8,128)(2,1)S(1)}, bf16[2,512,128]{2,1,0:T(8,128)(2,1)}, u32[]{:S(2)}) copy-start(bf16[2,512,128]{2,1,0:T(8,128)(2,1)} %copy-done.12) | copy-start | bytes 786436
  108.0 13.4 %copy-start.11 = (bf16[2,512,128]{2,1,0:T(8,128)(2,1)S(1)}, bf16[2,512,128]{2,1,0:T(8,128)(2,1)}, u32[]{:S(2)}) copy-start(bf16[2,512,128]{2,1,0:T(8,128)(2,1)} %copy-done.10) | copy-start | bytes 786436
  114.7 9.9 %copy-start.9 = (bf16[2,512,128]{2,1,0:T(8,128)(2,1)S(1)}, bf16[2,512,128]{2,1,0:T(8,128)(2,1)}, u32[]{:S(2)}) copy-start(bf16[2,512,128]{2,1,0:T(8,128)(2,1)} %copy-done.8) | copy-start | bytes 786436
  121.4 5.2 %copy-start.7 = (bf16[2,512,128]{2,1,0:T(8,128)(2,1)S(1)}, bf16[2,512,128]{2,1,0:T(8,128)(2,1)}, u32[]{:S(2)}) copy-start(bf16[2,512,128]{2,1,0:T(8,128)(2,1)} %copy-done.6) | copy-start | bytes 786436
  126.6 4.0 %slice-start.2 = ((s8[8388608]{0:T(1024)(128)(4,1)}), s8[4194304]{0:T(1024)(128)(4,1)S(1)}, s32[]{:S(2)}) async-start(s8[8388608]{0:T(1024)(128)(4,1)} %bitcast.360), calls=%async_computation.2 | async-start | bytes 8388608
  126.6 4.0 %copy-start.3 = (f32[128,512,8]{1,0,2:T(8,128)S(1)}, f32[128,512,8]{1,0,2:T(8,128)}, u32[]{:S(2)}) copy-start(f32[128,512,8]{1,0,2:T(8,128)} %fusion.44) | copy-start | bytes 6291460
  126.6 4.0 %copy-start.4 = (f32[128,512,8]{1,0,2:T(8,128)S(1)}, f32[128,512,8]{1,0,2:T(8,128)}, u32[]{:S(2)}) copy-start(f32[128,512,8]{1,0,2:T(8,128)} %fusion.42) | copy-start | bytes 6291460
  126.6 4.0 %copy-start.5 = (f32[128,512,8]{1,0,2:T(8,128)S(1)}, f32[128,512,8]{1,0,2:T(8,128)}, u32[]{:S(2)}) copy-start(f32[128,512,8]{1,0,2:T(8,128)} %fusion.40) | copy-start | bytes 6291460
  126.7 4.0 %copy-start.19 = (f32[512,8]{0,1:T(8,128)S(1)}, f32[512,8]{0,1:T(8,128)}, u32[]{:S(2)}) copy-start(f32[512,8]{0,1:T(8,128)} %get-tuple-element.20) | copy-start | bytes 49156
  128.6 3.5 %slice-start.3 = ((s8[8388608]{0:T(1024)(128)(4,1)}), s8[4194304]{0:T(1024)(128)(4,1)S(1)}, s32[]{:S(2)}) async-start(s8[8388608]{0:T(1024)(128)(4,1)} %bitcast.360), calls=%async_computation.3 | async-start | bytes 8388608
  128.6 3.5 %copy-start.18 = (bf16[2,512,128]{2,1,0:T(8,128)(2,1)S(1)}, bf16[2,512,128]{2,1,0:T(8,128)(2,1)}, u32[]{:S(2)}) copy-start(bf16[2,512,128]{2,1,0:T(8,128)(2,1)} %copy-done.17) | copy-start | bytes 786436
  130.6 8.9 %copy-start.1 = (bf16[512,1024]{1,0:T(8,128)(2,1)S(1)}, bf16[512,1024]{1,0:T(8,128)(2,1)}, u32[]{:S(2)}) copy-start(bf16[512,1024]{1,0:T(8,128)(2,1)} %param.4) | copy-start | bytes 3145732
where the time goes:
time: 140 us
  matrix products  55.2 us (39%)
  waiting for transfers between devices  36.4 us (26%)
  other arithmetic  24 us (17%)
  starting transfers between devices  16 us (11%)
  local copies, waits for them, and re-layouts  7.03 us (5%)
    ppermute x7, waiting for transfers between devices, passed_along(): return lax.ppermute(shard, axis, pairs)  36.4 us
    dot_general x8, matrix products, block_update(): jnp.einsum('rhgt,thd->rhgd', weights, piece_values, preferred_element_typ...  31 us
    dot_general x8, matrix products, on_device(): jnp.einsum('rhgd,thd->rhgt', query_head_rows, piece_keys, preferred_eleme...  24.1 us
    reduce_sum x4, other arithmetic, block_update(): total = total * correct + jnp.sum(probs, axis=-1)  22.2 us
    ppermute x7, starting transfers between devices, passed_along(): return lax.ppermute(shard, axis, pairs)  16 us
    unnamed x48, local copies, waits for them, and re-layouts  4.77 us
  transfers between devices with their start and end apart: 7, of which 6 were waited for; matrix products, arithmetic and copies ran while one was open for 17% of the time, Pallas kernels for 0%

commit v1 on v0

v1 whole, which is shorter than its diff:
```python
import functools
import math

import jax
import jax.numpy as jnp
from jax import lax
from jax.experimental import pallas as pl
from jax.experimental.pallas import tpu as pltpu
from jax.sharding import PartitionSpec as P

HEAD = 128
HEADS = 8
ROWS = 512
TILE = 256
UNROLL = 8
SCALE = math.log2(math.e) / math.sqrt(HEAD)
HUGE = 3.0e38
MESH = pl.DeviceIdType.MESH
F32 = jnp.float32
BF16 = jnp.bfloat16

OWN, NEAR, SWAP, SIDE, FAR, O_NEAR, O_SWAP, O_SIDE, EXTRA = range(9)
UP, ACROSS, SWAPPED, UP_TWO, ACROSS_TWO, S_NEAR, S_SWAP, S_SIDE, S_EXTRA = range(9)


def kernel(
    z_count, q_ref, k_ref, v_ref, span_ref, o_ref, kt, vb, *rest
):
    accs, maxes = rest[:UNROLL], rest[UNROLL : 2 * UNROLL]
    send_sem, recv_sem = rest[2 * UNROLL :]
    ctx = lax.axis_index("ctx")
    tp = lax.axis_index("tp")
    core = lax.rem(ctx, 2)
    column = lax.rem(ctx // 2, 2)
    z = ctx // 4
    has_down = z > 0
    has_up = z < z_count - 1
    up = (jnp.minimum(ctx + 4, 4 * z_count - 1), tp)
    down = (jnp.maximum(ctx - 4, 0), tp)
    across = (ctx + 2 - 4 * column, tp)
    sibling = (ctx + 1 - 2 * core, tp)

    barrier = pltpu.get_barrier_semaphore()
    pl.semaphore_signal(barrier, inc=1, device_id=across, device_id_type=MESH)
    pl.semaphore_signal(barrier, inc=1, device_id=sibling, device_id_type=MESH)

    @pl.when(has_down)
    def _():
        pl.semaphore_signal(barrier, inc=1, device_id=down, device_id_type=MESH)

    @pl.when(has_up)
    def _():
        pl.semaphore_signal(barrier, inc=1, device_id=up, device_id_type=MESH)

    kt[OWN] = k_ref[...].T
    vb[OWN] = v_ref[...]
    pl.semaphore_wait(barrier, 2 + has_down.astype(jnp.int32) + has_up.astype(jnp.int32))

    def copies(flow, source, target, device):
        return [
            pltpu.make_async_remote_copy(
                src_ref=ref.at[source],
                dst_ref=ref.at[target],
                send_sem=send_sem.at[flow, n],
                recv_sem=recv_sem.at[flow, n],
                device_id=device,
                device_id_type=MESH,
            )
            for n, ref in enumerate((kt, vb))
        ]

    go_up = copies(UP, OWN, NEAR, up)
    go_across = copies(ACROSS, OWN, SIDE, across)
    go_swapped = copies(SWAPPED, NEAR, SWAP, across)
    go_up_two = copies(UP_TWO, NEAR, FAR, up)
    go_across_two = copies(ACROSS_TWO, FAR, SIDE, across)
    go_near = copies(S_NEAR, NEAR, O_NEAR, sibling)
    go_swap = copies(S_SWAP, SWAP, O_SWAP, sibling)
    go_side = copies(S_SIDE, SIDE, O_SIDE, sibling)
    own_to_sibling = copies(S_EXTRA, OWN, EXTRA, sibling)
    far_to_sibling = copies(S_EXTRA, FAR, EXTRA, sibling)

    sends_up_two = has_down & has_up & ((column == 1) | (core == 1))
    gets_far = (z >= 2) & ((column == 1) | (core == 1))
    sends_across_two = (z >= 2) & (column == 1)
    gets_side_two = (z >= 2) & (column == 0)
    gets_side = (column == 1) | (z >= 2)

    @pl.when(core == 0)
    def _():
        for copy in own_to_sibling:
            copy.start()

    for n in range(2):

        @pl.when(has_up)
        def _():
            go_up[n].start()

        @pl.when(column == 0)
        def _():
            go_across[n].start()

    limit = span_ref[0]
    ones = jnp.ones((ROWS, HEAD), BF16)

    def weigh(scores, top):
        pieces = [
            jnp.exp2(scores[:, c : c + HEAD] * SCALE - top).astype(BF16)
            for c in range(0, scores.shape[1], HEAD)
        ]
        return jnp.concatenate(pieces, axis=1)

    def lanes_max(scores):
        best = scores[:, :HEAD]
        for c in range(HEAD, scores.shape[1], HEAD):
            best = jnp.maximum(best, scores[:, c : c + HEAD])
        return best

    def queries(tile):
        head, part = tile // (ROWS // TILE), lax.rem(tile, ROWS // TILE)
        return q_ref[
            pl.ds(pl.multiple_of(part * TILE, TILE), TILE),
            pl.ds(pl.multiple_of(head * HEAD, HEAD), HEAD),
        ]

    def with_ones(block, upto=ROWS):
        return jnp.concatenate([vb[block, :upto], ones[:upto]], axis=1)

    steps = HEADS * ROWS // TILE // UNROLL

    def own_block():
        rows = lax.broadcasted_iota(jnp.int32, (TILE, TILE), 0)
        cols = lax.broadcasted_iota(jnp.int32, (TILE, TILE), 1)

        @pl.loop(0, steps)
        def _(step):
            place = pl.ds(pl.multiple_of(step * TILE, TILE), TILE)
            for u in range(UNROLL):
                part = u % (ROWS // TILE)
                q = queries(step * UNROLL + u)
                upto = (part + 1) * TILE
                scores = jnp.dot(q, kt[OWN, :, :upto], preferred_element_type=F32)
                last = jnp.where(rows >= cols, scores[:, upto - TILE :], -jnp.inf)
                if part:
                    scores = jnp.concatenate([scores[:, : upto - TILE], last], axis=1)
                else:
                    scores = last
                top = jnp.max(lanes_max(scores), axis=1, keepdims=True) * SCALE
                top = jnp.broadcast_to(top, (TILE, HEAD))
                accs[u][place, :] = jnp.dot(
                    weigh(scores, top), with_ones(OWN, upto), preferred_element_type=F32
                )
                maxes[u][place, :] = top

    def attend(blocks):
        admitted = [j <= limit for _, j in blocks]

        @pl.loop(0, steps)
        def _(step):
            place = pl.ds(pl.multiple_of(step * TILE, TILE), TILE)
            for u in range(UNROLL):
                q = queries(step * UNROLL + u)
                before = maxes[u][place, :]
                all_scores = [
                    jnp.dot(q, kt[block], preferred_element_type=F32) for block, _ in blocks
                ]
                best = None
                for scores, fits in zip(all_scores, admitted):
                    mine = jnp.where(fits, lanes_max(scores), -jnp.inf)
                    best = mine if best is None else jnp.maximum(best, mine)
                best = jnp.max(best, axis=1, keepdims=True) * SCALE
                top = jnp.maximum(before, best)
                correct = jnp.exp2(before - top)
                acc = accs[u][place, :] * jnp.concatenate([correct, correct], axis=1)
                for (block, _), scores, fits in zip(blocks, all_scores, admitted):
                    acc += jnp.dot(
                        weigh(scores, jnp.where(fits, top, HUGE)),
                        with_ones(block),
                        preferred_element_type=F32,
                    )
                accs[u][place, :] = acc
                maxes[u][place, :] = top

    def wait_recv(flow):
        for copy in flow:
            copy.wait_recv()

    def pass_on(*flows):
        for pair in zip(*flows):
            for copy in pair:
                copy.start()

    def distance(chips):
        return 2 * chips, 2 * chips - 1 + 2 * core

    own_block()

    for n in range(2):

        @pl.when(has_down)
        def _():
            go_up[n].wait_recv()
            go_swapped[n].start()
            go_near[n].start()

        @pl.when(sends_up_two)
        def _():
            go_up_two[n].start()

    @pl.when(column == 1)
    def _():
        wait_recv(go_across)
        pass_on(go_side)

    @pl.when(core == 1)
    def _():
        wait_recv(own_to_sibling)
        attend([(EXTRA, 1)])

    @pl.when(has_down)
    def _():
        wait_recv(go_near)
        mine, other = distance(2)
        attend([(NEAR, mine), (O_NEAR, other)])

    @pl.when(gets_far)
    def _():
        wait_recv(go_up_two)

    @pl.when(sends_across_two)
    def _():
        pass_on(go_across_two)

    @pl.when((z >= 2) & (core == 1))
    def _():
        pass_on(far_to_sibling)

    @pl.when(has_down)
    def _():
        wait_recv(go_swapped)
        pass_on(go_swap)
        wait_recv(go_swap)
        mine, other = distance(1 + 2 * column)
        attend([(SWAP, mine), (O_SWAP, other)])

    @pl.when(gets_side_two)
    def _():
        wait_recv(go_across_two)
        pass_on(go_side)

    @pl.when((z >= 2) & (core == 0))
    def _():
        wait_recv(far_to_sibling)
        attend([(EXTRA, 7)])

    @pl.when(gets_side)
    def _():
        wait_recv(go_side)
        mine, other = distance(3 - 2 * column)
        attend([(SIDE, mine), (O_SIDE, other)])

    for step in range(steps):
        for u in range(UNROLL):
            tile = step * UNROLL + u
            head, part = divmod(tile, ROWS // TILE)
            acc = accs[u][step * TILE : (step + 1) * TILE, :]
            o_ref[part * TILE : (part + 1) * TILE, head * HEAD : (head + 1) * HEAD] = (
                acc[:, :HEAD] / acc[:, HEAD:]
            ).astype(BF16)

    for when, flow in (
        (has_up, go_up),
        (column == 0, go_across),
        (has_down, go_swapped),
        (sends_up_two, go_up_two),
        (sends_across_two, go_across_two),
        (has_down, go_near),
        (has_down, go_swap),
        (gets_side, go_side),
        (core == 0, own_to_sibling),
        ((z >= 2) & (core == 1), far_to_sibling),
    ):

        @pl.when(when)
        def _(flow=flow):
            for copy in flow:
                copy.wait_send()


def on_device(z_count, queries, keys, values, spans):
    vmem = pl.BlockSpec(memory_space=pltpu.VMEM)
    per_tile = HEADS * ROWS // UNROLL
    return pl.pallas_call(
        functools.partial(kernel, z_count),
        out_shape=jax.ShapeDtypeStruct(queries.shape, BF16),
        in_specs=[vmem, vmem, vmem, pl.BlockSpec(memory_space=pltpu.SMEM)],
        out_specs=vmem,
        scratch_shapes=[
            pltpu.VMEM((9, HEAD, ROWS), BF16),
            pltpu.VMEM((9, ROWS, HEAD), BF16),
        ]
        + [pltpu.VMEM((per_tile, 2 * HEAD), F32)] * UNROLL
        + [pltpu.VMEM((per_tile, HEAD), F32)] * UNROLL
        + [pltpu.SemaphoreType.DMA((9, 2)), pltpu.SemaphoreType.DMA((9, 2))],
        compiler_params=pltpu.CompilerParams(
            collective_id=1, has_side_effects=True, vmem_limit_bytes=56 * 2**20
        ),
    )(queries, keys, values, spans)


def solution(mesh):
    placed = (P("ctx", "tp"), P("ctx", "tp"), P("ctx", "tp"), P("ctx"))
    return jax.shard_map(
        functools.partial(on_device, mesh.shape["ctx"] // 4),
        mesh=mesh,
        in_specs=placed,
        out_specs=P("ctx", "tp"),
        check_vma=False,
    )
```

time: 140 us -> 45.3 us (0.32)
  the two profiles are of different devices: /device:TPU:142 before, /device:TPU:192 now
where the time goes in v1:
time: 45.3 us; the launch traced here: 45 us
  Pallas kernels  42 us (93%)
  local copies, waits for them, and re-layouts  2.26 us (5%)
  between operations  0.66 us (1%)
    pallas_call x1, Pallas kernels, on_device(): pl.pallas_call(functools.partial(kernel, z_count), out_shape=jax.ShapeDty...  42 us
    unnamed x1, local copies, waits for them, and re-layouts  2.26 us

profile of v1, /device:TPU:192, one launch (start us, length us, event | category | flops | bytes accessed | tf_op | source)
XLA Modules:
  0.0 45.0 jit_solution(5215712800519268547)
XLA Ops:
  0.7 42.0 %shard_map.46 = bf16[512,1024]{1,0:T(8,128)(2,1)} custom-call(bf16[512,1024]{1,0:T(8,128)(2,1)} %q_ref.1, bf16[512,128]{1,0:T(8,128)(2,1)} %k_ref.1, bf16[512,128]{1,0:T(8,128)(2,1)} %v_ref.1, s32[1]{0:T(128)S(6)} %copy.6.span_ref), custom_call_target="tpu_custom_call" | custom-call | tf_op jit(solution)/shard_map/pallas_call | solution.py:294
  42.7 2.3 %copy.7 = bf16[512,1024]{1,0:T(8,128)(2,1)} copy(bf16[512,1024]{1,0:T(8,128)(2,1)} %shard_map.46) | data formatting | bytes 2097152

commit v2 on v1

v2 whole, which is shorter than its diff:
```python
import functools
import math

import jax
import jax.numpy as jnp
from jax import lax
from jax.experimental import pallas as pl
from jax.experimental.pallas import tpu as pltpu
from jax.sharding import PartitionSpec as P

HEAD = 128
HEADS = 8
ROWS = 512
TILE = 256
TILES = HEADS * ROWS // TILE
SCALE = math.log2(math.e) / math.sqrt(HEAD)
HUGE = 3.0e38
MESH = pl.DeviceIdType.MESH
F32 = jnp.float32
BF16 = jnp.bfloat16

OWN, ONE, TWO, THREE, FAR, O_ONE, O_TWO, O_THREE, EXTRA = range(9)
UP, ACROSS, SWAPPED, UP_TWO, ACROSS_FAR, UP_ONE, S_ONE, S_TWO, S_THREE, S_EXTRA = range(10)


def kernel(
    z_count, q_hbm, k_hbm, v_hbm, span_ref, o_ref, q_ref, k_ref, kt, vb, acc_ref, max_ref,
    send_sem, recv_sem, load_sem
):
    ctx = lax.axis_index("ctx")
    tp = lax.axis_index("tp")
    core = lax.rem(ctx, 2)
    column = lax.rem(ctx // 2, 2)
    z = ctx // 4
    has_down = z > 0
    has_up = z < z_count - 1
    up = (jnp.minimum(ctx + 4, 4 * z_count - 1), tp)
    down = (jnp.maximum(ctx - 4, 0), tp)
    across = (ctx + 2 - 4 * column, tp)
    sibling = (ctx + 1 - 2 * core, tp)

    loads = [
        pltpu.make_async_copy(source, target, load_sem.at[n])
        for n, (source, target) in enumerate(
            ((k_hbm, k_ref), (v_hbm, vb.at[OWN]), (q_hbm, q_ref))
        )
    ]
    for load in loads:
        load.start()

    barrier = pltpu.get_barrier_semaphore()

    pl.semaphore_signal(barrier, inc=1, device_id=across, device_id_type=MESH)
    pl.semaphore_signal(barrier, inc=1, device_id=sibling, device_id_type=MESH)

    @pl.when(has_down)
    def _():
        pl.semaphore_signal(barrier, inc=1, device_id=down, device_id_type=MESH)

    @pl.when(has_up)
    def _():
        pl.semaphore_signal(barrier, inc=1, device_id=up, device_id_type=MESH)

    loads[0].wait()
    kt[OWN] = k_ref[...].T
    loads[1].wait()
    loads[2].wait()

    def copies(flow, source, target, device):
        return [
            pltpu.make_async_remote_copy(
                src_ref=ref.at[source],
                dst_ref=ref.at[target],
                send_sem=send_sem.at[flow, n],
                recv_sem=recv_sem.at[flow, n],
                device_id=device,
                device_id_type=MESH,
            )
            for n, ref in enumerate((kt, vb))
        ]

    go_up = copies(UP, OWN, TWO, up)
    go_across = copies(ACROSS, OWN, ONE, across)
    go_swapped = copies(SWAPPED, TWO, jnp.where(column == 0, THREE, ONE), across)
    go_up_two = copies(UP_TWO, TWO, FAR, up)
    go_across_far = copies(ACROSS_FAR, FAR, THREE, across)
    go_up_one = copies(UP_ONE, ONE, THREE, up)
    go_one = copies(S_ONE, ONE, O_ONE, sibling)
    go_two = copies(S_TWO, TWO, O_TWO, sibling)
    go_three = copies(S_THREE, THREE, O_THREE, sibling)
    own_to_sibling = copies(S_EXTRA, OWN, EXTRA, sibling)
    far_to_sibling = copies(S_EXTRA, FAR, EXTRA, sibling)

    has_far = z >= 2
    sends_up_two = has_down & has_up & (core == 1)
    sends_across_far = has_far & (column == 1) & (core == 1)
    sends_up_one = has_down & has_up & (column == 0) & (core == 0)
    has_one = (column == 1) | has_down
    has_three = jnp.where(column == 1, has_down, has_far)

    limit = span_ref[0]
    ones = jnp.ones((ROWS, HEAD), BF16)

    def weigh(scores, top):
        pieces = [
            jnp.exp2(scores[:, c : c + HEAD] * SCALE - top).astype(BF16)
            for c in range(0, scores.shape[1], HEAD)
        ]
        return jnp.concatenate(pieces, axis=1)

    def lanes_max(scores):
        best = scores[:, :HEAD]
        for c in range(HEAD, scores.shape[1], HEAD):
            best = jnp.maximum(best, scores[:, c : c + HEAD])
        return best

    def queries(tile):
        head, part = divmod(tile, ROWS // TILE)
        return q_ref[part * TILE : (part + 1) * TILE, head * HEAD : (head + 1) * HEAD]

    def finish(tile, acc):
        head, part = divmod(tile, ROWS // TILE)
        o_ref[part * TILE : (part + 1) * TILE, head * HEAD : (head + 1) * HEAD] = (
            acc[:, :HEAD] / acc[:, HEAD:]
        ).astype(BF16)

    def with_ones(block, upto=ROWS):
        return jnp.concatenate([vb[block, :upto], ones[:upto]], axis=1)

    def own_block(tiles):
        rows = lax.broadcasted_iota(jnp.int32, (TILE, TILE), 0)
        cols = lax.broadcasted_iota(jnp.int32, (TILE, TILE), 1)
        for tile in tiles:
            part = tile % (ROWS // TILE)
            upto = (part + 1) * TILE
            scores = jnp.dot(queries(tile), kt[OWN, :, :upto], preferred_element_type=F32)
            last = jnp.where(rows >= cols, scores[:, upto - TILE :], -jnp.inf)
            if part:
                scores = jnp.concatenate([scores[:, : upto - TILE], last], axis=1)
            else:
                scores = last
            top = jnp.max(lanes_max(scores), axis=1, keepdims=True) * SCALE
            top = jnp.broadcast_to(top, (TILE, HEAD))
            acc_ref[tile] = jnp.dot(
                weigh(scores, top), with_ones(OWN, upto), preferred_element_type=F32
            )
            max_ref[tile] = top

    def attend(blocks, last=False):
        admitted = [j <= limit for _, j in blocks]
        for tile in range(TILES):
            q = queries(tile)
            before = max_ref[tile]
            all_scores = [
                jnp.dot(q, kt[block], preferred_element_type=F32) for block, _ in blocks
            ]
            best = None
            for scores, fits in zip(all_scores, admitted):
                mine = jnp.where(fits, lanes_max(scores), -jnp.inf)
                best = mine if best is None else jnp.maximum(best, mine)
            best = jnp.max(best, axis=1, keepdims=True) * SCALE
            top = jnp.maximum(before, best)
            correct = jnp.exp2(before - top)
            acc = acc_ref[tile] * jnp.concatenate([correct, correct], axis=1)
            for (block, _), scores, fits in zip(blocks, all_scores, admitted):
                acc += jnp.dot(
                    weigh(scores, jnp.where(fits, top, HUGE)),
                    with_ones(block),
                    preferred_element_type=F32,
                )
            if last:
                finish(tile, acc)
            else:
                acc_ref[tile] = acc
                max_ref[tile] = top

    def wait_recv(flow):
        for copy in flow:
            copy.wait_recv()

    def pass_on(*flows):
        for pair in zip(*flows):
            for copy in pair:
                copy.start()

    def distance(chips):
        return 2 * chips, 2 * chips - 1 + 2 * core

    own_block(range(TILES // 2))
    pl.semaphore_wait(
        barrier, 2 + sum(some.astype(jnp.int32) for some in (has_down, has_up))
    )

    @pl.when(core == 0)
    def _():
        for copy in own_to_sibling:
            copy.start()

    for n in range(2):

        @pl.when(has_up)
        def _():
            go_up[n].start()

        @pl.when(column == 0)
        def _():
            go_across[n].start()

    own_block(range(TILES // 2, TILES))

    @pl.when(core == 1)
    def _():
        wait_recv(own_to_sibling)
        attend([(EXTRA, 1)])

    for n in range(2):

        @pl.when(has_down)
        def _():
            go_up[n].wait_recv()
            go_two[n].start()
            go_swapped[n].start()

        @pl.when(sends_up_two)
        def _():
            go_up_two[n].start()

    @pl.when(column == 1)
    def _():
        wait_recv(go_across)
        pass_on(go_one)

    @pl.when(has_down)
    def _():
        wait_recv(go_two)
        mine, other = distance(2)
        attend([(TWO, mine), (O_TWO, other)])
        wait_recv(go_swapped)

    @pl.when(has_down & (column == 0))
    def _():
        pass_on(go_one)

    @pl.when(sends_up_one)
    def _():
        pass_on(go_up_one)

    @pl.when(has_far & (core == 1))
    def _():
        wait_recv(go_up_two)

    @pl.when(sends_across_far)
    def _():
        pass_on(go_across_far)

    @pl.when(has_far & (core == 1))
    def _():
        pass_on(far_to_sibling)

    @pl.when(has_down & (column == 1))
    def _():
        pass_on(go_three)

    @pl.when(has_one)
    def _():
        wait_recv(go_one)
        mine, other = distance(1)
        attend([(ONE, mine), (O_ONE, other)])

    @pl.when(has_far & (column == 0) & (core == 0))
    def _():
        wait_recv(go_up_one)

    @pl.when(has_far & (column == 0) & (core == 1))
    def _():
        wait_recv(go_across_far)

    @pl.when(has_far & (column == 0))
    def _():
        pass_on(go_three)

    @pl.when(has_far & (core == 0))
    def _():
        wait_recv(far_to_sibling)
        attend([(EXTRA, 7)])

    @pl.when(has_three)
    def _():
        wait_recv(go_three)
        mine, other = distance(3)
        attend([(THREE, mine), (O_THREE, other)], last=True)

    @pl.when(jnp.logical_not(has_three))
    def _():
        for tile in range(TILES):
            finish(tile, acc_ref[tile])

    for when, flow in (
        (has_up, go_up),
        (column == 0, go_across),
        (has_down, go_swapped),
        (sends_up_two, go_up_two),
        (sends_across_far, go_across_far),
        (sends_up_one, go_up_one),
        (has_one, go_one),
        (has_down, go_two),
        (has_three, go_three),
        (core == 0, own_to_sibling),
        (has_far & (core == 1), far_to_sibling),
    ):

        @pl.when(when)
        def _(flow=flow):
            for copy in flow:
                copy.wait_send()


def on_device(z_count, queries, keys, values, spans):
    shape = jax.ShapeDtypeStruct(queries.shape, BF16)
    return pl.pallas_call(
        functools.partial(kernel, z_count),
        out_shape=shape,
        in_specs=[pl.BlockSpec(memory_space=pltpu.HBM)] * 3 + [pl.BlockSpec(memory_space=pltpu.SMEM)],
        out_specs=pl.BlockSpec(memory_space=pltpu.VMEM),
        scratch_shapes=[
            pltpu.VMEM(queries.shape, BF16),
            pltpu.VMEM(keys.shape, BF16),
            pltpu.VMEM((9, HEAD, ROWS), BF16),
            pltpu.VMEM((9, ROWS, HEAD), BF16),
            pltpu.VMEM((TILES, TILE, 2 * HEAD), F32),
            pltpu.VMEM((TILES, TILE, HEAD), F32),
            pltpu.SemaphoreType.DMA((10, 2)),
            pltpu.SemaphoreType.DMA((10, 2)),
            pltpu.SemaphoreType.DMA((3,)),
        ],
        compiler_params=pltpu.CompilerParams(
            collective_id=1, has_side_effects=True, vmem_limit_bytes=52 * 2**20
        ),
    )(queries, keys, values, spans)


def solution(mesh):
    placed = (P("ctx", "tp"), P("ctx", "tp"), P("ctx", "tp"), P("ctx"))
    return jax.shard_map(
        functools.partial(on_device, mesh.shape["ctx"] // 4),
        mesh=mesh,
        in_specs=placed,
        out_specs=P("ctx", "tp"),
        check_vma=False,
    )
```

time: 45.3 us -> 39.8 us (0.88)
  Pallas kernels: 42 us -> 36.2 us
  local copies, waits for them, and re-layouts: 2.26 us -> 2.77 us
    pallas_call x1, Pallas kernels: 42 us -> 36.2 us  [on_device(): pl.pallas_call(functools.partial(kernel, z_count), out_shape=shape, in_sp...]
    unnamed x1 -> x5, local copies, waits for them, and re-layouts: 2.26 us -> 2.77 us
where the time goes in v2:
time: 39.8 us; the launch traced here: 39.6 us
  Pallas kernels  36.2 us (91%)
  local copies, waits for them, and re-layouts  2.77 us (7%)
  between operations  0.67 us (2%)
    pallas_call x1, Pallas kernels, on_device(): pl.pallas_call(functools.partial(kernel, z_count), out_shape=shape, in_sp...  36.2 us
    unnamed x5, local copies, waits for them, and re-layouts  2.77 us

profile of v2, /device:TPU:192, one launch (start us, length us, event | category | flops | bytes accessed | tf_op | source)
XLA Modules:
  0.0 39.6 jit_solution(15246502758887834905)
XLA Ops:
  0.7 0.0 copy-start
  0.7 0.9 %copy-done = bf16[512,128]{1,0:T(8,128)(2,1)S(1)} copy-done((bf16[512,128]{1,0:T(8,128)(2,1)S(1)}, bf16[512,128]{1,0:T(8,128)(2,1)}, u32[]{:S(2)}) %copy-start) | copy-done | bytes 131096
  1.6 0.0 copy-start.1
  1.6 0.9 %copy-done.1 = bf16[512,128]{1,0:T(8,128)(2,1)S(1)} copy-done((bf16[512,128]{1,0:T(8,128)(2,1)S(1)}, bf16[512,128]{1,0:T(8,128)(2,1)}, u32[]{:S(2)}) %copy-start.1) | copy-done | bytes 131096
  2.5 36.2 %shard_map.46 = bf16[512,1024]{1,0:T(8,128)(2,1)S(1)} custom-call(bf16[512,1024]{1,0:T(8,128)(2,1)} %q_hbm.1, bf16[512,128]{1,0:T(8,128)(2,1)S(1)} %copy-done, bf16[512,128]{1,0:T(8,128)(2,1)S(1)} %copy-done.1, s32[1]{0:T(128)S(6)} %copy.6.span_ref), custom_call_target="tpu_custom_call" | custom-call | tf_op jit(solution)/shard_map/pallas_call | solution.py:320
  38.6 1.0 %copy.7 = bf16[512,1024]{1,0:T(8,128)(2,1)} copy(bf16[512,1024]{1,0:T(8,128)(2,1)S(1)} %shard_map.46) | data formatting | bytes 2097152
Async XLA Ops:
  0.7 0.9 %copy-start = (bf16[512,128]{1,0:T(8,128)(2,1)S(1)}, bf16[512,128]{1,0:T(8,128)(2,1)}, u32[]{:S(2)}) copy-start(bf16[512,128]{1,0:T(8,128)(2,1)} %k_hbm.1) | copy-start | bytes 393220
  1.6 0.9 %copy-start.1 = (bf16[512,128]{1,0:T(8,128)(2,1)S(1)}, bf16[512,128]{1,0:T(8,128)(2,1)}, u32[]{:S(2)}) copy-start(bf16[512,128]{1,0:T(8,128)(2,1)} %v_hbm.1) | copy-start | bytes 393220

commit v3 on v2

--- a/solution.py
+++ b/solution.py
@@ -317,6 +317,9 @@
 
 def on_device(z_count, queries, keys, values, spans):
     shape = jax.ShapeDtypeStruct(queries.shape, BF16)
+    queries, keys, values = (
+        pltpu.with_memory_space_constraint(array, pltpu.HBM) for array in (queries, keys, values)
+    )
     return pl.pallas_call(
         functools.partial(kernel, z_count),
         out_shape=shape,

time: 39.8 us -> 37.9 us (0.952)
  local copies, waits for them, and re-layouts: 2.77 us -> 0.97 us
    unnamed x5 -> x1, local copies, waits for them, and re-layouts: 2.77 us -> 0.97 us
where the time goes in v3:
time: 37.9 us; the launch traced here: 37.8 us
  Pallas kernels  36.1 us (95%)
  local copies, waits for them, and re-layouts  0.97 us (3%)
  between operations  0.66 us (2%)
    pallas_call x1, Pallas kernels, on_device(): pl.pallas_call(functools.partial(kernel, z_count), out_shape=shape, in_sp...  36.1 us
    unnamed x1, local copies, waits for them, and re-layouts  0.97 us

profile of v3, /device:TPU:192, one launch (start us, length us, event | category | flops | bytes accessed | tf_op | source)
XLA Modules:
  0.0 37.8 jit_solution(2863659401965401131)
XLA Ops:
  0.7 36.1 %shard_map.46 = bf16[512,1024]{1,0:T(8,128)(2,1)S(1)} custom-call(bf16[512,1024]{1,0:T(8,128)(2,1)} %q_hbm.1, bf16[512,128]{1,0:T(8,128)(2,1)} %k_hbm.1, bf16[512,128]{1,0:T(8,128)(2,1)} %v_hbm.1, s32[1]{0:T(128)S(6)} %copy.6.span_ref), custom_call_target="tpu_custom_call" | custom-call | tf_op jit(solution)/shard_map/pallas_call | solution.py:323
  36.8 1.0 %copy.7 = bf16[512,1024]{1,0:T(8,128)(2,1)} copy(bf16[512,1024]{1,0:T(8,128)(2,1)S(1)} %shard_map.46) | data formatting | bytes 2097152

commit v4 on v3

--- a/solution.py
+++ b/solution.py
@@ -235,6 +235,21 @@
         wait_recv(go_two)
         mine, other = distance(2)
         attend([(TWO, mine), (O_TWO, other)])
+
+    @pl.when(has_far & (core == 1))
+    def _():
+        wait_recv(go_up_two)
+
+    @pl.when(sends_across_far)
+    def _():
+        pass_on(go_across_far)
+
+    @pl.when(has_far & (core == 1))
+    def _():
+        pass_on(far_to_sibling)
+
+    @pl.when(has_down)
+    def _():
         wait_recv(go_swapped)
 
     @pl.when(has_down & (column == 0))
@@ -245,26 +260,24 @@
     def _():
         pass_on(go_up_one)
 
-    @pl.when(has_far & (core == 1))
-    def _():
-        wait_recv(go_up_two)
-
-    @pl.when(sends_across_far)
-    def _():
-        pass_on(go_across_far)
-
-    @pl.when(has_far & (core == 1))
-    def _():
-        pass_on(far_to_sibling)
-
     @pl.when(has_down & (column == 1))
     def _():
         pass_on(go_three)
 
+    gets_extra = has_far & (core == 0)
+    mine, other = distance(1)
+
     @pl.when(has_one)
     def _():
         wait_recv(go_one)
-        mine, other = distance(1)
+
+    @pl.when(gets_extra)
+    def _():
+        wait_recv(far_to_sibling)
+        attend([(ONE, mine), (O_ONE, other), (EXTRA, 7)])
+
+    @pl.when(has_one & jnp.logical_not(gets_extra))
+    def _():
         attend([(ONE, mine), (O_ONE, other)])
 
     @pl.when(has_far & (column == 0) & (core == 0))
@@ -278,11 +291,6 @@
     @pl.when(has_far & (column == 0))
     def _():
         pass_on(go_three)
-
-    @pl.when(has_far & (core == 0))
-    def _():
-        wait_recv(far_to_sibling)
-        attend([(EXTRA, 7)])
 
     @pl.when(has_three)
     def _():

time: 37.9 us -> 39.5 us (1.042)
  the two profiles are of different devices: /device:TPU:192 before, /device:TPU:167 now
where the time goes in v4:
time: 39.5 us; the launch traced here: 39.4 us
  Pallas kernels  37.8 us (96%)
  local copies, waits for them, and re-layouts  0.97 us (2%)
  between operations  0.66 us (2%)
    pallas_call x1, Pallas kernels, on_device(): pl.pallas_call(functools.partial(kernel, z_count), out_shape=shape, in_sp...  37.8 us
    unnamed x1, local copies, waits for them, and re-layouts  0.97 us

profile of v4, /device:TPU:167, one launch (start us, length us, event | category | flops | bytes accessed | tf_op | source)
XLA Modules:
  0.0 39.4 jit_solution(3732634087718795994)
XLA Ops:
  0.7 37.8 %shard_map.46 = bf16[512,1024]{1,0:T(8,128)(2,1)S(1)} custom-call(bf16[512,1024]{1,0:T(8,128)(2,1)} %q_hbm.1, bf16[512,128]{1,0:T(8,128)(2,1)} %k_hbm.1, bf16[512,128]{1,0:T(8,128)(2,1)} %v_hbm.1, s32[1]{0:T(128)S(6)} %copy.6.span_ref), custom_call_target="tpu_custom_call" | custom-call | tf_op jit(solution)/shard_map/pallas_call | solution.py:331
  38.4 1.0 %copy.7 = bf16[512,1024]{1,0:T(8,128)(2,1)} copy(bf16[512,1024]{1,0:T(8,128)(2,1)S(1)} %shard_map.46) | data formatting | bytes 2097152
